TPU v7x, 256 devices: a whole 4x4x8 slice. The times are simulated.
256 devices in a mesh: dp: 16 (over x, z_lo, core), hid: 16 (over y, z_hi).
Axes of the slice: x: 4, y: 4, z: 8 (z_hi: 4, z_lo: 2; z = z_hi * 2 + z_lo), core: 2. Of those that a mesh axis runs over, the one named last changes fastest.
Arguments:
- tokens: bfloat16 [6144, 4096], P(('dp', 'hid')), may hold values from -6 to 6
- cotangent: bfloat16 [6144, 4096], P(('dp', 'hid')), may hold values from -6 to 6
- w_in: bfloat16 [16, 128, 128, 128], P(None, 'hid'), may hold values from -0.1875 to 0.1875
- w_out: bfloat16 [16, 128, 128, 128], P(None, 'hid'), may hold values from -0.09375 to 0.09375
- block_index: int32 [16, 128], P(None, 'hid'), may hold values from 0 to 31, as said below
- live_count: int32 [128], P('hid'), may hold values from 2 to 16, as said below
Outputs:
- mixed: bfloat16 [6144, 4096], P(('dp', 'hid'))
- token_grad: bfloat16 [6144, 4096], P(('dp', 'hid'))
- in_grad: float32 [16, 128, 128, 128], P('dp', 'hid')
- out_grad: float32 [16, 128, 128, 128], P('dp', 'hid')
Inputs may be any that keep to these rules, and one draw needn't show every extreme that they name: For k < live_count[c] the numbers block_index[k, c] of one hidden block c are distinct; the other entries are not read. `live_count`: some hidden block has all 16 slots live.
All inputs are finite; a program needn't handle non-finite values.
Results may differ from a plain program's by a relative error of at most 0.02.
Values may be sent and summed in bfloat16 or wider, within the bound.
A program may use at most 128 MiB of HBM per device.

v0:
```python
import math

import jax
import jax.numpy as jnp
from jax import lax
from jax.sharding import PartitionSpec as P

gelu_root = 0.7978845608028654
gelu_cubic = 0.044715


def gelu_parts(pre):
    argument = gelu_root * (pre + gelu_cubic * pre * pre * pre)
    tangent = jnp.tanh(argument)
    activated = 0.5 * pre * (1.0 + tangent)
    slope = 0.5 * (1.0 + tangent) + 0.5 * pre * (1.0 - tangent * tangent) * gelu_root * (
        1.0 + 3.0 * gelu_cubic * pre * pre
    )
    return (activated, slope)


def body(tokens, cotangent, w_in, w_out, block_index, live_count):
    slot_count = w_in.shape[0]
    columns = w_in.shape[1]
    block_size = w_in.shape[2]
    local_rows = tokens.shape[0]
    feature_width = tokens.shape[1]
    feature_blocks = feature_width // block_size
    hid_size = lax.axis_size("hid")
    data_size = lax.axis_size("dp")
    grad_scale = 1.0 / math.sqrt(local_rows * hid_size * data_size)
    active = lax.broadcasted_iota(jnp.int32, (slot_count, columns), 0) < live_count[None, :]
    target = jnp.where(active, block_index, feature_blocks)
    selection_mask = (
        target[:, :, None]
        == lax.broadcasted_iota(jnp.int32, (slot_count, columns, feature_blocks), 2)
    ).astype(jnp.bfloat16)
    placed_out = jnp.einsum(
        "kcb,kcnm->cnbm", selection_mask, w_out, preferred_element_type=jnp.float32
    )
    placed_out = placed_out.astype(jnp.bfloat16).reshape(columns * block_size, feature_width)
    inbound_placement = jnp.einsum(
        "kcb,kcin->cnbi", selection_mask, w_in, preferred_element_type=jnp.float32
    )
    inbound_placement = inbound_placement.astype(jnp.bfloat16).reshape(
        columns * block_size, feature_width
    )
    whole_in, whole_back = (
        lax.all_gather(tokens, "hid", axis=0, tiled=True),
        lax.all_gather(cotangent, "hid", axis=0, tiled=True),
    )
    grouped_token_rows = whole_in.shape[0]
    picked = jnp.take(
        whole_in.reshape(grouped_token_rows, feature_blocks, block_size),
        target,
        axis=1,
        mode="fill",
        fill_value=0,
    )
    picked_back = jnp.take(
        whole_back.reshape(grouped_token_rows, feature_blocks, block_size),
        target,
        axis=1,
        mode="fill",
        fill_value=0,
    )
    pre = jnp.einsum("tkci,kcin->tcn", picked, w_in, preferred_element_type=jnp.float32)
    activated, slope = gelu_parts(pre)
    hidden = activated.astype(jnp.bfloat16)
    hidden_flat = hidden.reshape(grouped_token_rows, columns * block_size)

    def spread_rows(source, placed):
        return jnp.dot(source, placed, preferred_element_type=jnp.float32)

    mixed = lax.psum_scatter(
        spread_rows(hidden_flat, placed_out).astype(jnp.bfloat16),
        "hid",
        scatter_dimension=0,
        tiled=True,
    )
    hidden_grad = jnp.einsum(
        "tkcm,kcnm->tcn", picked_back, w_out, preferred_element_type=jnp.float32
    )
    pre_grad = (hidden_grad * slope).astype(jnp.bfloat16)
    pre_grad_flat = pre_grad.reshape(grouped_token_rows, columns * block_size)
    token_grad = lax.psum_scatter(
        spread_rows(pre_grad_flat, inbound_placement).astype(jnp.bfloat16),
        "hid",
        scatter_dimension=0,
        tiled=True,
    )
    stacked = lax.psum_scatter(
        jnp.stack(
            [
                jnp.einsum("tkci,tcn->kcin", picked, pre_grad, preferred_element_type=jnp.float32)
                * grad_scale,
                jnp.einsum(
                    "tcn,tkcm->kcnm", hidden, picked_back, preferred_element_type=jnp.float32
                )
                * grad_scale,
            ],
            axis=1,
        ).astype(jnp.bfloat16),
        "dp",
        scatter_dimension=0,
        tiled=True,
    ).astype(jnp.float32)
    in_shard = stacked[:, 0]
    out_shard = stacked[:, 1]
    return (mixed, token_grad, in_shard, out_shard)


def solution(mesh):
    in_specs = (
        P(("dp", "hid"), None),
        P(("dp", "hid"), None),
        P(None, "hid", None, None),
        P(None, "hid", None, None),
        P(None, "hid"),
        P("hid"),
    )
    out_specs = (
        P(("dp", "hid"), None),
        P(("dp", "hid"), None),
        P("dp", "hid", None, None),
        P("dp", "hid", None, None),
    )
    return jax.shard_map(body, mesh=mesh, in_specs=in_specs, out_specs=out_specs, check_vma=False)
```

profile of v0, /device:TPU:4, one launch (start us, length us, event | category | flops | bytes accessed | tf_op | source)
XLA Modules:
  0.0 620.3 jit_solution(10049232567896846754)
XLA Ops:
  9.7 71.4 %all-gather.3.cloned.1.call-done = bf16[384,4096]{1,0:T(8,128)(2,1)} async-done(((bf16[24,4096]{1,0:T(8,128)(2,1)}), bf16[384,4096]{1,0:T(8,128)(2,1)}) %all-gather.3.cloned.1.call-update) | async-done | bytes 3145744 | tf_op jit(solution)/shard_map/all_gather | solution.py:49
  81.1 4.7 copy.54
  85.8 3.5 copy.56
  89.3 60.0 %all-gather.5.cloned.1.call-done = bf16[384,4096]{1,0:T(8,128)(2,1)} async-done(((bf16[24,4096]{1,0:T(8,128)(2,1)}), bf16[384,4096]{1,0:T(8,128)(2,1)}) %all-gather.5.cloned.1.call-update) | async-done | bytes 3145744 | tf_op jit(solution)/shard_map/all_gather | solution.py:50
  149.3 4.7 copy.60
  154.0 4.7 copy.62
  158.6 8.3 %gather_fusion = bf16[128,384,128]{2,1,0:T(8,128)(2,1)} fusion(bf16[384,32,128]{2,0,1:T(8,128)(2,1)S(1)} %copy.56, s32[1024]{0:T(1024)S(1)} %pad_clamp_fusion), kind=kCustom, calls=%fused_computation.clone | custom fusion | bytes 25166336 | tf_op jit(solution)/shard_map/jit(_take)/gather | solution.py:53
  166.9 10.1 %gather_fusion.1 = bf16[128,384,128]{2,1,0:T(8,128)(2,1)} fusion(bf16[384,32,128]{2,0,1:T(8,128)(2,1)} %copy.62, s32[1024]{0:T(1024)S(1)} %pad_clamp_fusion), kind=kCustom, calls=%fused_computation.1.clone | custom fusion | bytes 25166336 | tf_op jit(solution)/shard_map/jit(_take)/gather | solution.py:60
  177.0 13.7 %select_bitcast_fusion = (bf16[384,16,8,128]{3,0,2,1:T(8,128)(2,1)}, bf16[384,16,8,128]{3,0,2,1:T(8,128)(2,1)S(1)}) fusion(bf16[16,8,384,128]{3,2,1,0:T(8,128)(2,1)} %bitcast.89, pred[16,8]{1,0:T(8,128)(4,1)S(1)} %copy.53, bf16[16,8,384,128]{3,2,1,0:T(8,128)(2,1)} %bitcast.88), kind=kLoop, calls=%fused_computation.6 | loop fusion | flops 12582912 | bytes 50331776 | tf_op jit(solution)/shard_map/jit(_take)/select_n | solution.py:60
  190.7 5.0 multiply_convert_fusion.2
  195.8 10.1 %fusion.30 = bf16[384,8,128]{0,2,1:T(8,128)(2,1)S(1)} fusion(f32[8,384,128,1]{1,2,0,3:T(8,128)} %get-tuple-element.28, bf16[384,16,8,128]{3,0,2,1:T(8,128)(2,1)} %get-tuple-element.25, bf16[16,8,128,128]{3,2,1,0:T(8,128)(2,1)} %param.11), kind=kOutput, calls=%fused_computation.33 | convolution fusion | flops 1618083840 | bytes 19136512 | tf_op jit(solution)/shard_map/tkcm,kcnm->tcn/dot_general | solution.py:81
  205.8 7.0 %fusion.16 = bf16[16,1,8,128,128]{3,4,0,2,1:T(8,128)(2,1)S(1)} fusion(bf16[384,16,8,128]{3,0,2,1:T(8,128)(2,1)} %copy-done, bf16[384,8,128]{0,2,1:T(8,128)(2,1)S(1)} %fusion.30), kind=kOutput, calls=%fused_computation.21 | convolution fusion | flops 1614807040 | bytes 17563648 | tf_op jit(solution)/shard_map/tkci,tcn->kcin/dot_general | solution.py:95
  212.8 8.5 %fusion.17 = bf16[16,1,8,128,128]{3,4,0,2,1:T(8,128)(2,1)} fusion(bf16[384,16,8,128]{3,0,2,1:T(8,128)(2,1)} %get-tuple-element.25, bf16[384,8,128]{0,2,1:T(8,128)(2,1)S(1)} %get-tuple-element.27), kind=kOutput, calls=%fused_computation.22 | convolution fusion | flops 1614807040 | bytes 17563648 | tf_op jit(solution)/shard_map/tcn,tkcm->kcnm/dot_general | solution.py:97
  221.3 6.2 pad_maximum_fusion
  227.8 8.9 %convert_bitcast_fusion = bf16[8,128,32,128]{1,2,3,0:T(8,128)(2,1)} fusion(bf16[16,8,128,128]{3,2,1,0:T(8,128)(2,1)} %param.10, s32[16,8]{0,1:T(8,128)S(1)} %get-tuple-element.22), kind=kOutput, calls=%fused_computation.17 | convolution fusion | flops 138416128 | bytes 12583424 | tf_op jit(solution)/shard_map/kcb,kcin->cnbi/dot_general | solution.py:42
  236.6 13.6 %copy.64 = bf16[8,128,32,128]{3,2,1,0:T(8,128)(2,1)} copy(bf16[8,128,32,128]{1,2,3,0:T(8,128)(2,1)} %convert_bitcast_fusion) | data formatting | bytes 16777216 | tf_op jit(solution)/shard_map/convert_element_type | solution.py:45
  250.2 9.2 %fusion.13 = bf16[384,4096]{1,0:T(8,128)(2,1)} fusion(bf16[384,1024]{0,1:T(8,128)(2,1)S(1)} %bitcast.95, bf16[128,8,32,128]{3,2,1,0:T(8,128)(2,1)} %bitcast.92), kind=kOutput, calls=%fused_computation.20 | convolution fusion | flops 3222798336 | bytes 12320768 | tf_op jit(solution)/shard_map/dot_general | solution.py:73
  259.7 5.7 convolution_convert_fusion
  265.4 12.1 %fusion.10 = bf16[384,4096]{1,0:T(8,128)(2,1)} fusion(bf16[384,1024]{0,1:T(8,128)(2,1)S(1)} %bitcast.94, bf16[128,8,32,128]{3,2,1,0:T(8,128)(2,1)S(1)} %bitcast.93), kind=kOutput, calls=%fused_computation.19 | convolution fusion | flops 3222798336 | bytes 12320768 | tf_op jit(solution)/shard_map/dot_general | solution.py:73
  278.2 145.4 %all-reduce.3.cloned.1.call-done = bf16[16,2,8,128,128]{3,4,0,2,1:T(8,128)(2,1)} async-done(((bf16[16,2,8,128,128]{3,4,0,2,1:T(8,128)(2,1)}), bf16[16,2,8,128,128]{3,4,0,2,1:T(8,128)(2,1)}) %all-reduce.3.cloned.1.call-update) | async-done | bytes 8388624
  423.6 1.8 dynamic-slice_convert_fusion
  425.5 1.0 copy.68
  427.5 92.8 %reduce-scatter.8.cloned.1.call-done = bf16[24,4096]{1,0:T(8,128)(2,1)} async-done(((bf16[384,4096]{1,0:T(8,128)(2,1)}), bf16[24,4096]{1,0:T(8,128)(2,1)}) %reduce-scatter.8.cloned.1.call-update) | async-done | bytes 196624 | tf_op jit(solution)/shard_map/reduce_scatter | solution.py:86
  520.3 93.5 %reduce-scatter.6.cloned.1.call-done = bf16[24,4096]{1,0:T(8,128)(2,1)} async-done(((bf16[384,4096]{1,0:T(8,128)(2,1)}), bf16[24,4096]{1,0:T(8,128)(2,1)}) %reduce-scatter.6.cloned.1.call-update) | async-done | bytes 196624 | tf_op jit(solution)/shard_map/reduce_scatter | solution.py:75
  (25 shorter events, 4.8 us)
Async XLA Ops:
  7.2 73.9 %all-gather.3.cloned.1.call-start = ((), (), s32[]{:S(2)}) async-start(), calls=%async_computation.2 | async-start | bytes 3342336 | tf_op jit(solution)/shard_map/all_gather | solution.py:49
  7.9 141.4 %all-gather.5.cloned.1.call-start = ((), (), s32[]{:S(2)}) async-start(), calls=%async_computation.4 | async-start | bytes 3342336 | tf_op jit(solution)/shard_map/all_gather | solution.py:50
  8.6 414.9 %all-reduce.3.cloned.1.call-start = ((), (), s32[]{:S(2)}) async-start(), calls=%async_computation.6 | async-start | bytes 16777216
  177.0 13.7 %copy-start.1 = (bf16[16,8,128,128]{3,2,1,0:T(8,128)(2,1)S(1)}, bf16[16,8,128,128]{3,2,1,0:T(8,128)(2,1)}, u32[]{:S(2)}) copy-start(bf16[16,8,128,128]{3,2,1,0:T(8,128)(2,1)} %param.10) | copy-start | bytes 12582916
  190.7 5.0 copy-start
  227.5 292.8 %reduce-scatter.8.cloned.1.call-start = ((), (), s32[]{:S(2)}) async-start(), calls=%async_computation.5 | async-start | bytes 3342336 | tf_op jit(solution)/shard_map/reduce_scatter | solution.py:86
  259.4 354.3 %reduce-scatter.6.cloned.1.call-start = ((), (), s32[]{:S(2)}) async-start(), calls=%async_computation.3 | async-start | bytes 3342336 | tf_op jit(solution)/shard_map/reduce_scatter | solution.py:75
  265.4 12.2 %copy-start.2 = (u32[256]{0:T(256)S(1)}, u32[256]{0:T(256)}, u32[]{:S(2)}) copy-start(u32[256]{0:T(256)} %constant.32) | copy-start | bytes 3076
Sparse Core Ops, SparseCore 0:
  10.5 70.5 all-gather.2
  83.6 65.7 all-gather.4
  227.6 195.9 all-reduce.2
  427.6 92.5 reduce-scatter.7
  524.3 89.3 reduce-scatter.5
where the time goes:
time: 621 us; the launch traced here: 620 us
  waiting for transfers between devices  464 us (75%)
  matrix products  66.4 us (11%)
  local copies, waits for them, and re-layouts  52.3 us (8%)
  other arithmetic  22.5 us (4%)
  between operations  13.9 us (2%)
    unnamed x6, waiting for transfers between devices  147 us
    reduce_scatter x1, waiting for transfers between devices, body(): lax.psum_scatter(spread_rows(hidden_flat, placed_out).astype(jnp.bfloat16...  93.5 us
    reduce_scatter x1, waiting for transfers between devices, body(): lax.psum_scatter(spread_rows(pre_grad_flat, inbound_placement).astype(jnp...  92.8 us
    all_gather x1, waiting for transfers between devices, body(): lax.all_gather(tokens, 'hid', axis=0, tiled=True)  71.4 us
    all_gather x1, waiting for transfers between devices, body(): lax.all_gather(cotangent, 'hid', axis=0, tiled=True)  60 us
    dot_general x2, matrix products, spread_rows(): return jnp.dot(source, placed, preferred_element_type=jnp.float32)  21.3 us
    select_n x1, other arithmetic, body(): jnp.take(whole_back.reshape(grouped_token_rows, feature_blocks, block_siz...  13.7 us
    convert_element_type x1, local copies, waits for them, and re-layouts, body(): inbound_placement.astype(jnp.bfloat16)  13.6 us
  transfers between devices with their start and end apart: 5, of which 5 were waited for; matrix products, arithmetic and copies ran while one was open for 10% of the time, Pallas kernels for 0%

commit v1 on v0

v1 whole, which is shorter than its diff:
```python
import functools
import math

import jax
import jax.numpy as jnp
from jax import lax
from jax.experimental import pallas as pl
from jax.experimental.pallas import tpu as pltpu
from jax.sharding import PartitionSpec as P

MESH = pl.DeviceIdType.MESH
gelu_root = 0.7978845608028654
gelu_cubic = 0.044715

BLK = 128
DB = 32
SLOTS = 16
COLS = 8
ROWS = 24
PAIR = 2 * ROWS
HALF = DB // 2
F32 = jnp.float32
BF16 = jnp.bfloat16

Z_FULL = (0, 1)
Z_HALF = (2, 3)
Y_FULL = ((4, 5), (8, 9), (12, 13), (16, 17))
Y_HALF = ((6, 7), (10, 11), (14, 15), (18, 19))
OY_HALF = ((20, 21), (24, 25), (28, 29), (32, 33))
OY_FULL = ((22, 23), (26, 27), (30, 31), (34, 35))
OZ_HALF = (36, 37)
OZ_FULL = (38, 39)
CORE = 40
XHALF = (48, 56)
XFULL = (64, 72)
ZLO = 80
COPIES = 88


def gelu_parts(pre):
    argument = gelu_root * (pre + gelu_cubic * pre * pre * pre)
    tangent = jnp.tanh(argument)
    activated = 0.5 * pre * (1.0 + tangent)
    slope = 0.5 * (1.0 + tangent) + 0.5 * pre * (1.0 - tangent * tangent) * gelu_root * (
        1.0 + 3.0 * gelu_cubic * pre * pre
    )
    return (activated, slope)


def kernel(
    grad_scale,
    slot_ref, live_ref, inverse_ref,
    tok_ref, cot_ref, w_in_ref, w_out_ref,
    mixed_ref, tgrad_ref, igrad_ref, ograd_ref,
    x0, x1, x2, x3,
    o0, o1, o2, o3,
    w_fwd, w_outz, w_inz, w_raw,
    hid, pgr, gmat,
    wg, core_in, xa, xb, xf1, xf2, zr,
    ya, yb, yf1, yf2, za, zb, zf1, zf2,
    load_sem, ssem, rsem,
):
    X = (x0, x1, x2, x3)
    O = (o0, o1, o2, o3)
    dp = lax.axis_index("dp")
    hd = lax.axis_index("hid")
    x, zl, core = dp // 4, lax.rem(dp // 2, 2), lax.rem(dp, 2)
    y, zh = hd // 4, lax.rem(hd, 4)

    def dev(dx=0, dzl=0, dcore=0, dy=0, dzh=0):
        return (
            lax.rem(x + dx + 4, 4) * 4 + lax.rem(zl + dzl, 2) * 2 + lax.rem(core + dcore, 2),
            lax.rem(y + dy + 4, 4) * 4 + lax.rem(zh + dzh + 4, 4),
        )

    zp, zm, yp, ym = dev(dzh=1), dev(dzh=-1), dev(dy=1), dev(dy=-1)
    xp, xm, other_zl, other_core = dev(dx=1), dev(dx=-1), dev(dzl=1), dev(dcore=1)

    def rcopy(src, dst, i, to):
        return pltpu.make_async_remote_copy(
            src_ref=src, dst_ref=dst, send_sem=ssem.at[i], recv_sem=rsem.at[i],
            device_id=to, device_id_type=MESH,
        )

    out_load = pltpu.make_async_copy(w_out_ref, w_outz.at[pl.ds(0, SLOTS)], load_sem.at[2])
    out_load.start()

    def in_load(k, slot):
        return pltpu.make_async_copy(w_in_ref.at[k], w_raw.at[slot], load_sem.at[slot])

    in_load(0, 0).start()

    barrier = pltpu.get_barrier_semaphore()
    peers = (zp, zm, yp, ym, xp, xm, other_zl, other_core)
    for p in peers:
        pl.semaphore_signal(barrier, inc=1, device_id=p, device_id_type=MESH)

    for b in range(DB):
        cols = pl.ds(b * BLK, BLK)
        both = jnp.concatenate(
            [tok_ref[:, cols].astype(F32), cot_ref[:, cols].astype(F32)], axis=0
        )
        x0[0, b] = both.astype(BF16)
    pl.semaphore_wait(barrier, len(peers))

    lo, hi = pl.ds(0, HALF), pl.ds(HALF, HALF)

    z_full = (
        rcopy(x0.at[0], x1.at[0], Z_FULL[0], zp),
        rcopy(x0.at[0], x2.at[0], Z_FULL[1], zm),
    )
    z_half = (
        rcopy(x1.at[0, lo], x3.at[0, lo], Z_HALF[0], zp),
        rcopy(x2.at[0, hi], x3.at[0, hi], Z_HALF[1], zm),
    )
    y_full = [
        (
            rcopy(X[j].at[0], X[j].at[1], Y_FULL[j][0], yp),
            rcopy(X[j].at[0], X[j].at[2], Y_FULL[j][1], ym),
        )
        for j in range(4)
    ]
    y_half = [
        (
            rcopy(X[j].at[1, lo], X[j].at[3, lo], Y_HALF[j][0], yp),
            rcopy(X[j].at[2, hi], X[j].at[3, hi], Y_HALF[j][1], ym),
        )
        for j in range(4)
    ]

    def start(pair):
        for c in pair:
            c.start()

    def arrived(pair):
        for c in pair:
            c.wait_recv()

    def forward_y(j):
        for full, half in zip(y_full[j], y_half[j]):
            full.wait_recv()
            half.start()

    def prepare(k, _):
        slot = lax.rem(k, 2)
        in_load(k, slot).wait()

        @pl.when(k + 1 < SLOTS)
        def _():
            in_load(k + 1, 1 - slot).start()

        for c in range(COLS):
            live = live_ref[k, c]
            wi = (w_raw[slot, c].astype(F32) * live).astype(BF16)
            wo = (w_outz[k, c].astype(F32) * live).astype(BF16)
            w_outz[k, c] = wo
            w_inz[k, c] = wi.T
            w_fwd[c, pl.ds(k * BLK, BLK), :] = jnp.concatenate([wi, wo.T], axis=1)
        return 0

    def forward(j):
        def one(c, _):
            lhs = jnp.concatenate(
                [X[j][:, slot_ref[k, c]].reshape(4 * PAIR, BLK) for k in range(SLOTS)], axis=1
            )
            acc = jnp.dot(lhs, w_fwd[c], preferred_element_type=F32)
            acc = acc.reshape(4, PAIR, 2 * BLK)
            pre = acc[:, :ROWS, :BLK]
            hidden_grad = acc[:, ROWS:, BLK:]
            activated, slope = gelu_parts(pre)
            pre_grad = hidden_grad * slope
            rows = pl.ds(j * 4 * ROWS, 4 * ROWS)
            hid[c, rows, :] = activated.reshape(4 * ROWS, BLK).astype(BF16)
            pgr[c, rows, :] = pre_grad.reshape(4 * ROWS, BLK).astype(BF16)
            zero = jnp.zeros_like(pre)
            both = jnp.concatenate(
                [
                    jnp.concatenate([pre_grad, zero], axis=2),
                    jnp.concatenate([zero, activated], axis=2),
                ],
                axis=1,
            )
            gmat[c, pl.ds(j * 4 * PAIR, 4 * PAIR), :] = both.reshape(4 * PAIR, 2 * BLK).astype(BF16)
            return 0

        lax.fori_loop(0, COLS, one, 0)

    start(z_full)
    start(y_full[0])
    w_outz[SLOTS] = jnp.zeros(w_outz.shape[1:], BF16)
    w_inz[SLOTS] = jnp.zeros(w_inz.shape[1:], BF16)
    out_load.wait()
    lax.fori_loop(0, SLOTS // 2, prepare, 0)
    forward_y(0)
    lax.fori_loop(SLOTS // 2, SLOTS, prepare, 0)
    for full, half in zip(z_full, z_half):
        full.wait_recv()
        half.start()
    start(y_full[1])
    start(y_full[2])
    arrived(y_half[0])
    forward(0)
    forward_y(1)
    arrived(z_half)
    start(y_full[3])
    forward_y(2)
    arrived(y_half[1])
    forward(1)
    arrived(y_half[2])
    forward(2)
    forward_y(3)
    arrived(y_half[3])
    forward(3)

    steps = (0, 3, 1, 2)

    def core_copy(c):
        return rcopy(wg.at[1, c], core_in.at[c], CORE + c, other_core)

    def x_half(c):
        return (
            rcopy(wg.at[0, c, 6], xa.at[c], XHALF[0] + c, xm),
            rcopy(wg.at[0, c, 7], xb.at[c], XHALF[1] + c, xp),
        )

    def x_full(c):
        return (
            rcopy(wg.at[0, c, pl.ds(2, 2)], xf1.at[c], XFULL[0] + c, xm),
            rcopy(wg.at[0, c, pl.ds(4, 2)], xf2.at[c], XFULL[1] + c, xp),
        )

    def z_low(c):
        return rcopy(wg.at[0, c, 1], zr.at[c], ZLO + c, other_zl)

    def weight_grad(c, _):
        left = gmat[c].T
        for rc in (1, 0):
            for rx in range(4):
                tiles, masks = [], []
                for rz in range(2):
                    k = (
                        lax.rem(x + steps[rx], 4) * 4
                        + lax.rem(zl + rz, 2) * 2
                        + lax.rem(core + rc, 2)
                    )
                    b = slot_ref[k, c]
                    tiles.append(
                        jnp.concatenate([X[j][:, b].reshape(4 * PAIR, BLK) for j in range(4)], axis=0)
                    )
                    masks.append(live_ref[k, c] * grad_scale)
                res = jnp.dot(left, jnp.concatenate(tiles, axis=1), preferred_element_type=F32)
                for rz in range(2):
                    wg[rc, c, rx * 2 + rz] = (
                        res[:, rz * BLK : (rz + 1) * BLK] * masks[rz]
                    ).astype(BF16)
            if rc == 1:
                core_copy(c).start()
        return 0

    def add_core(c):
        core_copy(c).wait_recv()
        for i in (6, 7, 2, 3, 4, 5, 0, 1):
            wg[0, c, i] = (wg[0, c, i].astype(F32) + core_in[c, i].astype(F32)).astype(BF16)
        start(x_half(c))

    def add_x_half(c):
        arrived(x_half(c))
        wg[0, c, 2] = (wg[0, c, 2].astype(F32) + xa[c].astype(F32)).astype(BF16)
        wg[0, c, 5] = (wg[0, c, 5].astype(F32) + xb[c].astype(F32)).astype(BF16)
        start(x_full(c))

    def add_x_full(c):
        arrived(x_full(c))
        wg[0, c, 1] = (
            wg[0, c, 1].astype(F32) + xf1[c, 1].astype(F32) + xf2[c, 1].astype(F32)
        ).astype(BF16)
        z_low(c).start()

    def finish(c):
        z_low(c).wait_recv()
        total = (
            wg[0, c, 0].astype(F32) + xf1[c, 0].astype(F32) + xf2[c, 0].astype(F32)
            + zr[c].astype(F32)
        )
        igrad_ref[0, c] = total[:BLK].T
        ograd_ref[0, c] = total[BLK:]

    def loop(f, first, last):
        def step(c, _):
            f(c)
            return 0

        lax.fori_loop(first, last, step, 0)

    lax.fori_loop(0, COLS, weight_grad, 0)
    loop(add_core, 0, COLS)

    def spread(q, _):
        def placed(source):
            return jnp.concatenate(
                [
                    jnp.concatenate(
                        [source[inverse_ref[c, 2 * q], c], source[inverse_ref[c, 2 * q + 1], c]],
                        axis=1,
                    )
                    for c in range(COLS)
                ],
                axis=0,
            )

        h = jnp.concatenate([hid[c] for c in range(COLS)], axis=1)
        g = jnp.concatenate([pgr[c] for c in range(COLS)], axis=1)
        m = jnp.dot(h, placed(w_outz), preferred_element_type=F32).reshape(16, ROWS, 2 * BLK)
        t = jnp.dot(g, placed(w_inz), preferred_element_type=F32).reshape(16, ROWS, 2 * BLK)
        both = jnp.concatenate([m, t], axis=1).astype(BF16)
        for j in range(4):
            for i in range(2):
                O[j][:, 2 * q + i] = both[4 * j : 4 * j + 4, :, i * BLK : (i + 1) * BLK]
        return 0

    lax.fori_loop(0, DB // 2, spread, 0)

    def add_blocks(dst, d, src, s, first, count):
        def step(i, _):
            at = pl.ds(first + i * 8, 8)
            frm = pl.ds(i * 8, 8)
            dst[d, at] = (dst[d, at].astype(F32) + src[s, frm].astype(F32)).astype(BF16)
            return 0

        lax.fori_loop(0, count // 8, step, 0)

    oy_half = [
        (
            rcopy(O[j].at[3, lo], ya.at[j], OY_HALF[j][0], ym),
            rcopy(O[j].at[3, hi], yb.at[j], OY_HALF[j][1], yp),
        )
        for j in range(4)
    ]
    oy_full = [
        (
            rcopy(O[j].at[1], yf1.at[j], OY_FULL[j][0], ym),
            rcopy(O[j].at[2], yf2.at[j], OY_FULL[j][1], yp),
        )
        for j in range(4)
    ]
    oz_half = (
        rcopy(o3.at[0, lo], za.at[0], OZ_HALF[0], zm),
        rcopy(o3.at[0, hi], zb.at[0], OZ_HALF[1], zp),
    )
    oz_full = (
        rcopy(o1.at[0], zf1.at[0], OZ_FULL[0], zm),
        rcopy(o2.at[0], zf2.at[0], OZ_FULL[1], zp),
    )

    def y_mid(j):
        oy_half[j][0].wait_recv()
        add_blocks(O[j], 1, ya, j, 0, HALF)
        oy_full[j][0].start()
        oy_half[j][1].wait_recv()
        add_blocks(O[j], 2, yb, j, HALF, HALF)
        oy_full[j][1].start()

    def y_end(j):
        arrived(oy_full[j])
        add_blocks(O[j], 0, yf1, j, 0, DB)
        add_blocks(O[j], 0, yf2, j, 0, DB)

    for j in (3, 1, 2, 0):
        start(oy_half[j])
    loop(add_x_half, 0, COLS)
    y_mid(3)
    y_mid(1)
    y_end(3)
    start(oz_half)
    y_mid(2)
    y_end(1)
    oz_half[0].wait_recv()
    add_blocks(o1, 0, za, 0, 0, HALF)
    oz_full[0].start()
    y_mid(0)
    y_end(2)
    oz_half[1].wait_recv()
    add_blocks(o2, 0, zb, 0, HALF, HALF)
    oz_full[1].start()
    loop(add_x_full, 0, COLS)
    y_end(0)
    loop(finish, 0, COLS)
    arrived(oz_full)
    for b in range(DB):
        total = o0[0, b].astype(F32) + zf1[0, b].astype(F32) + zf2[0, b].astype(F32)
        cols = pl.ds(b * BLK, BLK)
        mixed_ref[:, cols] = total[:ROWS].astype(BF16)
        tgrad_ref[:, cols] = total[ROWS:].astype(BF16)

    for pair in (z_full, z_half, *y_full, *y_half, *oy_half, *oy_full, oz_half, oz_full):
        for c in pair:
            c.wait_send()

    def sent(c):
        core_copy(c).wait_send()
        for r in (*x_half(c), *x_full(c)):
            r.wait_send()
        z_low(c).wait_send()

    loop(sent, 0, COLS)


def body(tokens, cotangent, w_in, w_out, block_index, live_count):
    slots, columns = block_index.shape
    grad_scale = 1.0 / math.sqrt(tokens.shape[0] * lax.axis_size("hid") * lax.axis_size("dp"))
    slot_number = lax.broadcasted_iota(jnp.int32, (slots, columns), 0)
    active = slot_number < live_count[None, :]
    slot = jnp.where(active, block_index, 0)
    hit = active[:, :, None] & (
        block_index[:, :, None] == lax.broadcasted_iota(jnp.int32, (slots, columns, DB), 2)
    )
    inverse = slots + jnp.sum(jnp.where(hit, slot_number[:, :, None] - slots, 0), axis=0)
    vmem = pl.BlockSpec(memory_space=pltpu.VMEM)
    smem = pl.BlockSpec(memory_space=pltpu.SMEM)
    hbm = pl.BlockSpec(memory_space=pl.ANY)
    shard = (4, DB, PAIR, BLK)
    half = (HALF, PAIR, BLK)
    full = (DB, PAIR, BLK)
    return pl.pallas_call(
        functools.partial(kernel, grad_scale),
        out_shape=(
            jax.ShapeDtypeStruct(tokens.shape, BF16),
            jax.ShapeDtypeStruct(tokens.shape, BF16),
            jax.ShapeDtypeStruct((1, COLS, BLK, BLK), F32),
            jax.ShapeDtypeStruct((1, COLS, BLK, BLK), F32),
        ),
        in_specs=[smem, smem, smem, vmem, vmem, hbm, hbm],
        out_specs=(vmem, vmem, vmem, vmem),
        scratch_shapes=[
            *[pltpu.VMEM(shard, BF16) for _ in range(8)],
            pltpu.VMEM((COLS, SLOTS * BLK, 2 * BLK), BF16),
            pltpu.VMEM((SLOTS + 1, COLS, BLK, BLK), BF16),
            pltpu.VMEM((SLOTS + 1, COLS, BLK, BLK), BF16),
            pltpu.VMEM((2, COLS, BLK, BLK), BF16),
            pltpu.VMEM((COLS, 16 * ROWS, BLK), BF16),
            pltpu.VMEM((COLS, 16 * ROWS, BLK), BF16),
            pltpu.VMEM((COLS, 16 * PAIR, 2 * BLK), BF16),
            pltpu.VMEM((2, COLS, 8, 2 * BLK, BLK), BF16),
            pltpu.VMEM((COLS, 8, 2 * BLK, BLK), BF16),
            pltpu.VMEM((COLS, 2 * BLK, BLK), BF16),
            pltpu.VMEM((COLS, 2 * BLK, BLK), BF16),
            pltpu.VMEM((COLS, 2, 2 * BLK, BLK), BF16),
            pltpu.VMEM((COLS, 2, 2 * BLK, BLK), BF16),
            pltpu.VMEM((COLS, 2 * BLK, BLK), BF16),
            pltpu.VMEM((4, *half), BF16),
            pltpu.VMEM((4, *half), BF16),
            pltpu.VMEM((4, *full), BF16),
            pltpu.VMEM((4, *full), BF16),
            pltpu.VMEM((1, *half), BF16),
            pltpu.VMEM((1, *half), BF16),
            pltpu.VMEM((1, *full), BF16),
            pltpu.VMEM((1, *full), BF16),
            pltpu.SemaphoreType.DMA((3,)),
            pltpu.SemaphoreType.DMA((COPIES,)),
            pltpu.SemaphoreType.DMA((COPIES,)),
        ],
        compiler_params=pltpu.CompilerParams(
            collective_id=0, has_side_effects=True, vmem_limit_bytes=62 * 2**20
        ),
        cost_estimate=pl.CostEstimate(
            flops=3 * 2 * 2 * 384 * 2048 * 1024, bytes_accessed=12 * 2**20, transcendentals=384 * 1024
        ),
    )(slot, active.astype(F32), inverse, tokens, cotangent, w_in, w_out)


def solution(mesh):
    in_specs = (
        P(("dp", "hid"), None),
        P(("dp", "hid"), None),
        P(None, "hid", None, None),
        P(None, "hid", None, None),
        P(None, "hid"),
        P("hid"),
    )
    out_specs = (
        P(("dp", "hid"), None),
        P(("dp", "hid"), None),
        P("dp", "hid", None, None),
        P("dp", "hid", None, None),
    )
    return jax.shard_map(body, mesh=mesh, in_specs=in_specs, out_specs=out_specs, check_vma=False)
```

time: 621 us -> 185 us (0.30)
  waiting for transfers between devices: 464 us -> 0 us
  Pallas kernels: 0 us -> 171 us
  matrix products: 66.4 us -> 0 us
  local copies, waits for them, and re-layouts: 52.3 us -> 7.73 us
  other arithmetic: 22.5 us -> 3.23 us
  between operations: 13.9 us -> 0.65 us
    reduce_scatter x2 -> x0, waiting for transfers between devices: 186 us -> none  [the longest x1 93.5 us: body(): lax.psum_scatter(spread_rows(hidden_flat, placed_out).astype(jnp.bfloat16...]
    pallas_call x0 -> x1, Pallas kernels: none -> 171 us  [body(): pl.pallas_call(functools.partial(kernel, grad_scale), out_shape=(jax.Shap...]
    unnamed x6 -> x0, waiting for transfers between devices: 147 us -> none
    all_gather x2 -> x0, waiting for transfers between devices: 131 us -> none  [the longest x1 71.4 us: body(): lax.all_gather(tokens, 'hid', axis=0, tiled=True)]
    dot_general x8 -> x0, matrix products: 66.4 us -> none  [the longest x2 21.3 us: spread_rows(): return jnp.dot(source, placed, preferred_element_type=jnp.float32)]
    gather x2 -> x0, local copies, waits for them, and re-layouts: 18.3 us -> none  [the longest x1 10.1 us: body(): jnp.take(whole_back.reshape(grouped_token_rows, feature_blocks, block_siz...]
    convert_element_type x1 -> x0, local copies, waits for them, and re-layouts: 13.6 us -> none  [body(): inbound_placement.astype(jnp.bfloat16)]
    select_n x2 -> x1, other arithmetic: 13.7 us -> 1.26 us  [body(): slot = jnp.where(active, block_index, 0)]
  transfers between devices with their start and end apart: 5 -> 0, of which waited for: 5 -> 0; matrix products, arithmetic and copies ran while one was open for 10% -> 0% of each run, Pallas kernels for 0% -> 0%
where the time goes in v1:
time: 185 us; the launch traced here: 183 us
  Pallas kernels  171 us (92%)
  local copies, waits for them, and re-layouts  7.73 us (4%)
  other arithmetic  3.23 us (2%)
    pallas_call x1, Pallas kernels, body(): pl.pallas_call(functools.partial(kernel, grad_scale), out_shape=(jax.Shap...  171 us
    unnamed x5, local copies, waits for them, and re-layouts  7.73 us

profile of v1, /device:TPU:4, one launch (start us, length us, event | category | flops | bytes accessed | tf_op | source)
XLA Modules:
  0.0 183.0 jit_solution(8873225173026394965)
XLA Ops:
  0.6 0.8 copy.12
  1.4 1.3 fusion.2.slot_ref
  2.7 1.3 iota_compare_fusion.1
  3.9 0.1 select_reduce_fusion
  4.0 0.6 broadcast_add_fusion.inverse_ref
  4.6 171.4 %shard_map.93 = (bf16[24,4096]{1,0:T(8,128)(2,1)}, bf16[24,4096]{1,0:T(8,128)(2,1)}, f32[1,8,128,128]{3,2,1,0:T(8,128)}, f32[1,8,128,128]{3,2,1,0:T(8,128)}) custom-call(s32[16,8]{1,0:T(8,128)} %fusion.2.slot_ref, f32[16,8]{1,0:T(8,128)} %get-tuple-element.5.live_ref, s32[8,32]{1,0:T(8,128)} %broadcast_add_fusion.inverse_ref, bf16[24,4096]{1,0:T(8,128)(2,1)} %tok_ref.1, ...), custom_call_target="tpu_custom_call" | custom-call | flops 9663676416 | bytes 12582912 | tf_op jit(solution)/shard_map/pallas_call | solution.py:424
  176.0 1.6 copy.18
  177.7 1.6 copy.19
  179.3 1.9 %copy.20 = f32[1,8,128,128]{3,2,1,0:T(8,128)} copy(f32[1,8,128,128]{3,2,1,0:T(8,128)} %get-tuple-element.12) | data formatting | bytes 1048576
  181.1 1.9 %copy.21 = f32[1,8,128,128]{3,2,1,0:T(8,128)} copy(f32[1,8,128,128]{3,2,1,0:T(8,128)} %get-tuple-element.13) | data formatting | bytes 1048576
  (1 shorter events, 0.0 us)

commit v2 on v0

v2 whole, which is shorter than its diff:
```python
import functools
import math

import jax
import jax.numpy as jnp
from jax import lax
from jax.experimental import pallas as pl
from jax.experimental.pallas import tpu as pltpu
from jax.sharding import PartitionSpec as P

MESH = pl.DeviceIdType.MESH
gelu_root = 0.7978845608028654
gelu_cubic = 0.044715

BLK = 128
DB = 32
SLOTS = 16
COLS = 8
ROWS = 24
PAIR = 2 * ROWS
HALF = DB // 2
F32 = jnp.float32
BF16 = jnp.bfloat16

GROUPS = (
    ((0, 0), (0, 1), (0, 2), (0, 3)),
    ((1, 0), (1, 1), (1, 2), (2, 0), (2, 1), (2, 2)),
    ((3, 0), (3, 1), (3, 2), (3, 3), (1, 3), (2, 3)),
)
PLACE = {jr: (g, i) for g, group in enumerate(GROUPS) for i, jr in enumerate(group)}
ORDER = {jr: n for n, jr in enumerate(jr for group in GROUPS for jr in group)}
FIRST = (0, 4, 10)
COPIES = 112


def gelu_parts(pre):
    argument = gelu_root * (pre + gelu_cubic * pre * pre * pre)
    tangent = jnp.tanh(argument)
    activated = 0.5 * pre * (1.0 + tangent)
    slope = 0.5 * (1.0 + tangent) + 0.5 * pre * (1.0 - tangent * tangent) * gelu_root * (
        1.0 + 3.0 * gelu_cubic * pre * pre
    )
    return (activated, slope)


def kernel(
    grad_scale,
    index_ref, count_ref,
    tok_ref, cot_ref, w_in_ref, w_out_ref,
    mixed_ref, tgrad_ref, igrad_ref, ograd_ref,
    x0, x1, x2, parts,
    w_fwd, w_outz, w_inz,
    hid, pgr, gmat,
    wg, core_in, xa, xb, xf1, xf2, zr,
    ya, yb, yf1, yf2, za, zb, zf1, zf2, zq1, zq2,
    inverse,
    load_sem, ssem, rsem,
):
    X = (x0, x1, x2)
    dp = lax.axis_index("dp")
    hd = lax.axis_index("hid")
    x, zl, core = dp // 4, lax.rem(dp // 2, 2), lax.rem(dp, 2)
    y, zh = hd // 4, lax.rem(hd, 4)

    def dev(dx=0, dzl=0, dcore=0, dy=0, dzh=0):
        return (
            lax.rem(x + dx + 4, 4) * 4 + lax.rem(zl + dzl, 2) * 2 + lax.rem(core + dcore, 2),
            lax.rem(y + dy + 4, 4) * 4 + lax.rem(zh + dzh + 4, 4),
        )

    zp, zm, yp, ym = dev(dzh=1), dev(dzh=-1), dev(dy=1), dev(dy=-1)
    xp, xm, other_zl, other_core = dev(dx=1), dev(dx=-1), dev(dzl=1), dev(dcore=1)

    copies = []
    numbers = iter(range(COPIES))

    def make(src, dst, i, to):
        return pltpu.make_async_remote_copy(
            src_ref=src, dst_ref=dst, send_sem=ssem.at[i], recv_sem=rsem.at[i],
            device_id=to, device_id_type=MESH,
        )

    def rcopy(src, dst, to):
        c = make(src, dst, next(numbers), to)
        copies.append(c)
        return c

    def start(pair):
        for c in pair:
            c.start()

    def arrived(pair):
        for c in pair:
            c.wait_recv()

    def live(k, c):
        return k < count_ref[c]

    def slot(k, c):
        return jnp.where(live(k, c), index_ref[c, k], 0)

    def mask(k, c):
        return jnp.where(live(k, c), 1.0, 0.0).astype(F32)

    def loop(f, first, last):
        def step(c, _):
            f(c)
            return 0

        lax.fori_loop(first, last, step, 0)

    def raw(k):
        return wg.at[k // 8, lax.rem(k, 8), :, pl.ds(0, BLK), :]

    def in_load(k):
        return pltpu.make_async_copy(w_in_ref.at[k], raw(k), load_sem.at[k])

    def out_load(k):
        return pltpu.make_async_copy(w_out_ref.at[k], w_outz.at[k], load_sem.at[SLOTS + k])

    barrier = pltpu.get_barrier_semaphore()
    peers = (zp, zm, yp, ym, xp, xm, other_zl, other_core)
    for p in peers:
        pl.semaphore_signal(barrier, inc=1, device_id=p, device_id_type=MESH)

    for b in range(DB):
        cols = pl.ds(b * BLK, BLK)
        both = jnp.concatenate(
            [tok_ref[:, cols].astype(F32), cot_ref[:, cols].astype(F32)], axis=0
        )
        x0[0, b] = both.astype(BF16)
    pl.semaphore_wait(barrier, len(peers))

    lo, hi = pl.ds(0, HALF), pl.ds(HALF, HALF)
    whole = pl.ds(0, DB)

    def shard(j, r, blocks=whole):
        g, i = PLACE[(j, r)]
        return X[g].at[i, blocks]

    def part(j, r, blocks=whole):
        return parts.at[ORDER[(j, r)], blocks]

    z_first = (
        rcopy(shard(0, 0, lo), shard(1, 0, lo), zp),
        rcopy(shard(0, 0, hi), shard(2, 0, hi), zm),
    )
    z_second = (
        rcopy(shard(0, 0, hi), shard(1, 0, hi), zp),
        rcopy(shard(0, 0, lo), shard(2, 0, lo), zm),
    )
    z_relay = (
        rcopy(shard(1, 0, lo), shard(3, 0, lo), zp),
        rcopy(shard(2, 0, hi), shard(3, 0, hi), zm),
    )
    z_cross = (
        rcopy(shard(0, 3), shard(1, 3), zp),
        rcopy(shard(0, 3), shard(2, 3), zm),
    )

    def both_ways(j, blocks):
        return (
            rcopy(shard(j, 0, blocks), shard(j, 1, blocks), yp),
            rcopy(shard(j, 0, blocks), shard(j, 2, blocks), ym),
        )

    def y_relay_of(j):
        return (
            rcopy(shard(j, 1, lo), shard(j, 3, lo), yp),
            rcopy(shard(j, 2, hi), shard(j, 3, hi), ym),
        )

    y_own = both_ways(0, whole)
    y_one = (both_ways(1, lo), both_ways(1, hi))
    y_two = (both_ways(2, hi), both_ways(2, lo))
    y_far = (both_ways(3, lo), both_ways(3, hi))
    y_relay_own = y_relay_of(0)
    y_relay_far = y_relay_of(3)

    def prepare(k):
        in_load(k).wait()
        out_load(k).wait()
        for c in range(COLS):
            m = mask(k, c)
            wi = (wg[k // 8, lax.rem(k, 8), c, :BLK, :].astype(F32) * m).astype(BF16)
            wo = (w_outz[k, c].astype(F32) * m).astype(BF16)
            w_outz[k, c] = wo
            w_inz[k, c] = wi.T
            w_fwd[c, pl.ds(k * BLK, BLK), :] = jnp.concatenate([wi, wo.T], axis=1)

    def invert(c):
        joined = [jnp.where(live(k, c), index_ref[c, k], -1) for k in range(SLOTS)]

        def one(b):
            found = jnp.int32(SLOTS)
            for k in range(SLOTS):
                found = jnp.where(joined[k] == b, k, found)
            inverse[c, b] = found

        loop(one, 0, DB)

    def forward(g):
        n = len(GROUPS[g])

        def one(c):
            lhs = jnp.concatenate(
                [X[g][:, slot(k, c)].reshape(n * PAIR, BLK) for k in range(SLOTS)], axis=1
            )
            acc = jnp.dot(lhs, w_fwd[c], preferred_element_type=F32)
            acc = acc.reshape(n, PAIR, 2 * BLK)
            pre = acc[:, :ROWS, :BLK]
            hidden_grad = acc[:, ROWS:, BLK:]
            activated, slope = gelu_parts(pre)
            pre_grad = hidden_grad * slope
            rows = pl.ds(FIRST[g] * ROWS, n * ROWS)
            hid[c, rows, :] = activated.reshape(n * ROWS, BLK).astype(BF16)
            pgr[c, rows, :] = pre_grad.reshape(n * ROWS, BLK).astype(BF16)
            zero = jnp.zeros_like(pre)
            both = jnp.concatenate(
                [
                    jnp.concatenate([pre_grad, zero], axis=2),
                    jnp.concatenate([zero, activated], axis=2),
                ],
                axis=1,
            )
            gmat[c, pl.ds(FIRST[g] * PAIR, n * PAIR), :] = both.reshape(n * PAIR, 2 * BLK).astype(BF16)

        loop(one, 0, COLS)

    def spread(first, count):
        rows = pl.ds(first * ROWS, count * ROWS)

        def one(q):
            def placed(source):
                return jnp.concatenate(
                    [
                        jnp.concatenate(
                            [source[inverse[c, 2 * q], c], source[inverse[c, 2 * q + 1], c]],
                            axis=1,
                        )
                        for c in range(COLS)
                    ],
                    axis=0,
                )

            h = jnp.concatenate([hid[c, rows, :] for c in range(COLS)], axis=1)
            g = jnp.concatenate([pgr[c, rows, :] for c in range(COLS)], axis=1)
            m = jnp.dot(h, placed(w_outz), preferred_element_type=F32)
            t = jnp.dot(g, placed(w_inz), preferred_element_type=F32)
            both = jnp.concatenate(
                [m.reshape(count, ROWS, 2 * BLK), t.reshape(count, ROWS, 2 * BLK)], axis=1
            ).astype(BF16)
            for i in range(2):
                parts[pl.ds(first, count), 2 * q + i] = both[:, :, i * BLK : (i + 1) * BLK]

        loop(one, 0, DB // 2)

    start(z_first)
    start(y_own)
    start(z_second)
    for k in range(SLOTS):
        in_load(k).start()
        out_load(k).start()
    w_outz[SLOTS] = jnp.zeros(w_outz.shape[1:], BF16)
    w_inz[SLOTS] = jnp.zeros(w_inz.shape[1:], BF16)
    loop(prepare, 0, SLOTS // 2)
    arrived(y_own)
    start(y_relay_own)
    arrived(z_first)
    start(z_relay)
    start(y_one[0])
    start(y_two[0])
    loop(prepare, SLOTS // 2, SLOTS)
    arrived(y_relay_own)
    start(z_cross)
    loop(invert, 0, COLS)
    arrived(z_second)
    start(y_one[1])
    start(y_two[1])
    forward(0)
    arrived(z_relay)
    start(y_far[0])
    start(y_far[1])
    for pair in (*y_one, *y_two):
        arrived(pair)
    forward(1)
    spread(0, 10)

    def add_blocks(dst, src, first, count):
        def step(i):
            at = pl.ds(first + i * 8, 8)
            frm = pl.ds(i * 8, 8)
            n = ORDER[dst]
            parts[n, at] = (parts[n, at].astype(F32) + src[frm].astype(F32)).astype(BF16)

        loop(step, 0, count // 8)

    oz_cross = (
        rcopy(part(1, 3), zq1.at[whole], zm),
        rcopy(part(2, 3), zq2.at[whole], zp),
    )
    oy_half = {
        j: (
            rcopy(part(j, 3, lo), ya.at[n], ym),
            rcopy(part(j, 3, hi), yb.at[n], yp),
        )
        for n, j in enumerate((0, 3))
    }
    oy_full = {
        j: (
            rcopy(part(j, 1), yf1.at[j], ym),
            rcopy(part(j, 2), yf2.at[j], yp),
        )
        for j in range(4)
    }
    oz_half = (
        rcopy(part(3, 0, lo), za.at[lo], zm),
        rcopy(part(3, 0, hi), zb.at[lo], zp),
    )
    oz_full = (
        rcopy(part(1, 0), zf1.at[whole], zm),
        rcopy(part(2, 0), zf2.at[whole], zp),
    )

    def y_mid(j):
        n = (0, 3).index(j)
        oy_half[j][0].wait_recv()
        add_blocks((j, 1), ya.at[n], 0, HALF)
        oy_full[j][0].start()
        oy_half[j][1].wait_recv()
        add_blocks((j, 2), yb.at[n], HALF, HALF)
        oy_full[j][1].start()

    def y_end(j):
        arrived(oy_full[j])
        add_blocks((j, 0), yf1.at[j], 0, DB)
        add_blocks((j, 0), yf2.at[j], 0, DB)

    y_far[0][0].wait_recv()
    y_relay_far[0].start()
    y_far[1][1].wait_recv()
    y_relay_far[1].start()
    start(oy_full[1])
    start(oy_full[2])
    y_far[0][1].wait_recv()
    y_far[1][0].wait_recv()
    arrived(z_cross)
    arrived(y_relay_far)
    forward(2)
    spread(10, 6)
    start(oz_cross)
    start(oy_half[3])

    steps = (0, 3, 1, 2)
    base = len(copies)
    CORE, XH1, XH2, XF1, XF2, ZLO = (base + 8 * i for i in range(6))

    def core_copy(c):
        return make(wg.at[1, c], core_in.at[c], CORE + c, other_core)

    def x_half(c):
        return (
            make(wg.at[0, c, 6], xa.at[c], XH1 + c, xm),
            make(wg.at[0, c, 7], xb.at[c], XH2 + c, xp),
        )

    def x_full(c):
        return (
            make(wg.at[0, c, pl.ds(2, 2)], xf1.at[c], XF1 + c, xm),
            make(wg.at[0, c, pl.ds(4, 2)], xf2.at[c], XF2 + c, xp),
        )

    def z_low(c):
        return make(wg.at[0, c, 1], zr.at[c], ZLO + c, other_zl)

    def add_core(c):
        core_copy(c).wait_recv()
        for i in (6, 7, 2, 3, 4, 5, 0, 1):
            wg[0, c, i] = (wg[0, c, i].astype(F32) + core_in[c, i].astype(F32)).astype(BF16)
        start(x_half(c))

    def add_x_half(c):
        arrived(x_half(c))
        wg[0, c, 2] = (wg[0, c, 2].astype(F32) + xa[c].astype(F32)).astype(BF16)
        wg[0, c, 5] = (wg[0, c, 5].astype(F32) + xb[c].astype(F32)).astype(BF16)
        start(x_full(c))

    def add_x_full(c):
        arrived(x_full(c))
        wg[0, c, 1] = (
            wg[0, c, 1].astype(F32) + xf1[c, 1].astype(F32) + xf2[c, 1].astype(F32)
        ).astype(BF16)
        z_low(c).start()

    def finish(c):
        z_low(c).wait_recv()
        total = (
            wg[0, c, 0].astype(F32) + xf1[c, 0].astype(F32) + xf2[c, 0].astype(F32)
            + zr[c].astype(F32)
        )
        igrad_ref[0, c] = total[:BLK].T
        ograd_ref[0, c] = total[BLK:]

    def weight_grad(c):
        left = gmat[c].T
        for rc in (1, 0):
            for rx in range(4):
                tiles, masks = [], []
                for rz in range(2):
                    k = (
                        lax.rem(x + steps[rx], 4) * 4
                        + lax.rem(zl + rz, 2) * 2
                        + lax.rem(core + rc, 2)
                    )
                    b = slot(k, c)
                    tiles.append(
                        jnp.concatenate(
                            [X[g][:, b].reshape(len(GROUPS[g]) * PAIR, BLK) for g in range(3)], axis=0
                        )
                    )
                    masks.append(mask(k, c) * grad_scale)
                res = jnp.dot(left, jnp.concatenate(tiles, axis=1), preferred_element_type=F32)
                for rz in range(2):
                    wg[rc, c, rx * 2 + rz] = (
                        res[:, rz * BLK : (rz + 1) * BLK] * masks[rz]
                    ).astype(BF16)
            if rc == 1:
                core_copy(c).start()

        @pl.when(c >= 1)
        def _():
            add_core(c - 1)

        @pl.when(c >= 4)
        def _():
            add_x_half(c - 4)

        @pl.when(c == 5)
        def _():
            y_mid(3)

    loop(weight_grad, 0, COLS)
    add_core(COLS - 1)
    loop(add_x_half, 4, COLS)
    y_end(1)
    y_end(2)
    arrived(oz_cross)
    add_blocks((0, 3), zq1, 0, DB)
    add_blocks((0, 3), zq2, 0, DB)
    start(oy_half[0])
    y_end(3)
    start(oz_half)
    loop(add_x_full, 0, 3)
    y_mid(0)
    oz_half[0].wait_recv()
    add_blocks((1, 0), za, 0, HALF)
    oz_full[0].start()
    oz_half[1].wait_recv()
    add_blocks((2, 0), zb, HALF, HALF)
    oz_full[1].start()
    loop(add_x_full, 3, COLS)
    y_end(0)
    loop(finish, 0, COLS)
    arrived(oz_full)
    for b in range(DB):
        total = parts[0, b].astype(F32) + zf1[b].astype(F32) + zf2[b].astype(F32)
        cols = pl.ds(b * BLK, BLK)
        mixed_ref[:, cols] = total[:ROWS].astype(BF16)
        tgrad_ref[:, cols] = total[ROWS:].astype(BF16)

    for c in copies:
        c.wait_send()

    def sent(c):
        core_copy(c).wait_send()
        for r in (*x_half(c), *x_full(c)):
            r.wait_send()
        z_low(c).wait_send()

    loop(sent, 0, COLS)


def hand_on(*refs):
    n = len(refs) // 2
    for i in range(n):
        refs[n + i][...] = refs[i][...]


def body(tokens, cotangent, w_in, w_out, block_index, live_count):
    grad_scale = 1.0 / math.sqrt(tokens.shape[0] * lax.axis_size("hid") * lax.axis_size("dp"))
    vmem = pl.BlockSpec(memory_space=pltpu.VMEM)
    smem = pl.BlockSpec(memory_space=pltpu.SMEM)
    hbm = pl.BlockSpec(memory_space=pl.ANY)
    half = (HALF, PAIR, BLK)
    full = (DB, PAIR, BLK)
    tile = (2 * BLK, BLK)
    shapes = (
        jax.ShapeDtypeStruct(tokens.shape, BF16),
        jax.ShapeDtypeStruct(tokens.shape, BF16),
        jax.ShapeDtypeStruct((1, COLS, BLK, BLK), F32),
        jax.ShapeDtypeStruct((1, COLS, BLK, BLK), F32),
    )
    results = pl.pallas_call(
        functools.partial(kernel, grad_scale),
        out_shape=shapes,
        in_specs=[smem, smem, vmem, vmem, hbm, hbm],
        out_specs=(vmem, vmem, vmem, vmem),
        scratch_shapes=[
            *[pltpu.VMEM((len(g), *full), BF16) for g in GROUPS],
            pltpu.VMEM((16, *full), BF16),
            pltpu.VMEM((COLS, SLOTS * BLK, 2 * BLK), BF16),
            pltpu.VMEM((SLOTS + 1, COLS, BLK, BLK), BF16),
            pltpu.VMEM((SLOTS + 1, COLS, BLK, BLK), BF16),
            pltpu.VMEM((COLS, 16 * ROWS, BLK), BF16),
            pltpu.VMEM((COLS, 16 * ROWS, BLK), BF16),
            pltpu.VMEM((COLS, 16 * PAIR, 2 * BLK), BF16),
            pltpu.VMEM((2, COLS, 8, *tile), BF16),
            pltpu.VMEM((COLS, 8, *tile), BF16),
            pltpu.VMEM((COLS, *tile), BF16),
            pltpu.VMEM((COLS, *tile), BF16),
            pltpu.VMEM((COLS, 2, *tile), BF16),
            pltpu.VMEM((COLS, 2, *tile), BF16),
            pltpu.VMEM((COLS, *tile), BF16),
            pltpu.VMEM((2, *half), BF16),
            pltpu.VMEM((2, *half), BF16),
            pltpu.VMEM((4, *full), BF16),
            pltpu.VMEM((4, *full), BF16),
            pltpu.VMEM(half, BF16),
            pltpu.VMEM(half, BF16),
            *[pltpu.VMEM(full, BF16) for _ in range(4)],
            pltpu.SMEM((COLS, DB), jnp.int32),
            pltpu.SemaphoreType.DMA((2 * SLOTS,)),
            pltpu.SemaphoreType.DMA((COPIES,)),
            pltpu.SemaphoreType.DMA((COPIES,)),
        ],
        compiler_params=pltpu.CompilerParams(
            collective_id=0, has_side_effects=True, vmem_limit_bytes=62 * 2**20
        ),
        cost_estimate=pl.CostEstimate(
            flops=3 * 2 * 2 * 384 * 2048 * 1024, bytes_accessed=12 * 2**20, transcendentals=384 * 1024
        ),
    )(block_index.T, live_count, tokens, cotangent, w_in, w_out)
    return pl.pallas_call(
        hand_on,
        out_shape=shapes,
        in_specs=[vmem] * len(shapes),
        out_specs=(vmem,) * len(shapes),
    )(*results)


def solution(mesh):
    in_specs = (
        P(("dp", "hid"), None),
        P(("dp", "hid"), None),
        P(None, "hid", None, None),
        P(None, "hid", None, None),
        P(None, "hid"),
        P("hid"),
    )
    out_specs = (
        P(("dp", "hid"), None),
        P(("dp", "hid"), None),
        P("dp", "hid", None, None),
        P("dp", "hid", None, None),
    )
    return jax.shard_map(body, mesh=mesh, in_specs=in_specs, out_specs=out_specs, check_vma=False)
```

time: 621 us -> 148 us (0.24)
  waiting for transfers between devices: 464 us -> 0 us
  Pallas kernels: 0 us -> 145 us
  matrix products: 66.4 us -> 0 us
  local copies, waits for them, and re-layouts: 52.3 us -> 0 us
  other arithmetic: 22.5 us -> 0 us
  between operations: 13.9 us -> 0.64 us
    reduce_scatter x2 -> x0, waiting for transfers between devices: 186 us -> none  [the longest x1 93.5 us: body(): lax.psum_scatter(spread_rows(hidden_flat, placed_out).astype(jnp.bfloat16...]
    unnamed x6 -> x0, waiting for transfers between devices: 147 us -> none
    pallas_call x0 -> x2, Pallas kernels: none -> 145 us  [the longest x1 143 us: body(): pl.pallas_call(functools.partial(kernel, grad_scale), out_shape=shapes, i...]
    all_gather x2 -> x0, waiting for transfers between devices: 131 us -> none  [the longest x1 71.4 us: body(): lax.all_gather(tokens, 'hid', axis=0, tiled=True)]
    dot_general x8 -> x0, matrix products: 66.4 us -> none  [the longest x2 21.3 us: spread_rows(): return jnp.dot(source, placed, preferred_element_type=jnp.float32)]
    gather x2 -> x0, local copies, waits for them, and re-layouts: 18.3 us -> none  [the longest x1 10.1 us: body(): jnp.take(whole_back.reshape(grouped_token_rows, feature_blocks, block_siz...]
    select_n x2 -> x0, other arithmetic: 13.7 us -> none  [the longest x1 13.7 us: body(): jnp.take(whole_back.reshape(grouped_token_rows, feature_blocks, block_siz...]
    convert_element_type x1 -> x0, local copies, waits for them, and re-layouts: 13.6 us -> none  [body(): inbound_placement.astype(jnp.bfloat16)]
  transfers between devices with their start and end apart: 5 -> 0, of which waited for: 5 -> 0; matrix products, arithmetic and copies ran while one was open for 10% -> 0% of each run, Pallas kernels for 0% -> 0%
where the time goes in v2:
time: 148 us; the launch traced here: 146 us
  Pallas kernels  145 us (98%)
    pallas_call x1, Pallas kernels, body(): pl.pallas_call(functools.partial(kernel, grad_scale), out_shape=shapes, i...  143 us

profile of v2, /device:TPU:4, one launch (start us, length us, event | category | flops | bytes accessed | tf_op | source)
XLA Modules:
  0.0 145.8 jit_solution(15169008123555230110)
XLA Ops:
  0.6 142.6 %shard_map.93 = (bf16[24,4096]{1,0:T(8,128)(2,1)}, bf16[24,4096]{1,0:T(8,128)(2,1)}, f32[1,8,128,128]{3,2,1,0:T(8,128)}, f32[1,8,128,128]{3,2,1,0:T(8,128)}) custom-call(s32[8,16]{1,0:T(8,128)} %bitcast.1, s32[8]{0:T(128)} %count_ref.1, bf16[24,4096]{1,0:T(8,128)(2,1)} %tok_ref.1, bf16[24,4096]{1,0:T(8,128)(2,1)} %cot_ref.1, ...), custom_call_target="tpu_custom_call" | custom-call | flops 9663676416 | bytes 12582912 | tf_op jit(solution)/shard_map/pallas_call | solution.py:503
  143.3 2.5 %shard_map.94 = (bf16[24,4096]{1,0:T(8,128)(2,1)}, bf16[24,4096]{1,0:T(8,128)(2,1)}, f32[1,8,128,128]{3,2,1,0:T(8,128)}, f32[1,8,128,128]{3,2,1,0:T(8,128)}) custom-call(bf16[24,4096]{1,0:T(8,128)(2,1)} %get-tuple-element.8.refs_0_, bf16[24,4096]{1,0:T(8,128)(2,1)} %get-tuple-element.9.refs_1_, f32[1,8,128,128]{3,2,1,0:T(8,128)} %get-tuple-element.10.refs_2_, ...), custom_call_target="tpu_custom_call" | custom-call | tf_op jit(solution)/shard_map/pallas_call | solution.py:543

commit v3 on v2

--- a/solution.py
+++ b/solution.py
@@ -30,7 +30,7 @@
 PLACE = {jr: (g, i) for g, group in enumerate(GROUPS) for i, jr in enumerate(group)}
 ORDER = {jr: n for n, jr in enumerate(jr for group in GROUPS for jr in group)}
 FIRST = (0, 4, 10)
-COPIES = 112
+COPIES = 120
 
 
 def gelu_parts(pre):
@@ -102,12 +102,12 @@
     def mask(k, c):
         return jnp.where(live(k, c), 1.0, 0.0).astype(F32)
 
-    def loop(f, first, last):
+    def loop(f, first, last, unroll=1):
         def step(c, _):
             f(c)
             return 0
 
-        lax.fori_loop(first, last, step, 0)
+        lax.fori_loop(first, last, step, 0, unroll=unroll)
 
     def raw(k):
         return wg.at[k // 8, lax.rem(k, 8), :, pl.ds(0, BLK), :]
@@ -225,9 +225,9 @@
             )
             gmat[c, pl.ds(FIRST[g] * PAIR, n * PAIR), :] = both.reshape(n * PAIR, 2 * BLK).astype(BF16)
 
-        loop(one, 0, COLS)
-
-    def spread(first, count):
+        loop(one, 0, COLS, 4)
+
+    def spread(first, count, q_first=0, q_last=DB // 2):
         rows = pl.ds(first * ROWS, count * ROWS)
 
         def one(q):
@@ -253,51 +253,60 @@
             for i in range(2):
                 parts[pl.ds(first, count), 2 * q + i] = both[:, :, i * BLK : (i + 1) * BLK]
 
-        loop(one, 0, DB // 2)
+        loop(one, q_first, q_last, 8)
 
     start(z_first)
     start(y_own)
-    start(z_second)
     for k in range(SLOTS):
         in_load(k).start()
         out_load(k).start()
     w_outz[SLOTS] = jnp.zeros(w_outz.shape[1:], BF16)
     w_inz[SLOTS] = jnp.zeros(w_inz.shape[1:], BF16)
     loop(prepare, 0, SLOTS // 2)
+    arrived(z_first)
+    start(z_second)
+    start(z_relay)
     arrived(y_own)
     start(y_relay_own)
-    arrived(z_first)
-    start(z_relay)
     start(y_one[0])
     start(y_two[0])
     loop(prepare, SLOTS // 2, SLOTS)
-    arrived(y_relay_own)
-    start(z_cross)
-    loop(invert, 0, COLS)
     arrived(z_second)
     start(y_one[1])
     start(y_two[1])
+    loop(invert, 0, COLS)
+    arrived(y_relay_own)
     forward(0)
     arrived(z_relay)
+    start(z_cross)
     start(y_far[0])
     start(y_far[1])
     for pair in (*y_one, *y_two):
         arrived(pair)
     forward(1)
-    spread(0, 10)
-
-    def add_blocks(dst, src, first, count):
+    spread(0, 10, 0, DB // 4)
+    y_far[0][0].wait_recv()
+    y_relay_far[0].start()
+    y_far[1][1].wait_recv()
+    y_relay_far[1].start()
+    spread(0, 10, DB // 4, DB // 2)
+
+    def add_blocks(dst, src, first, count, other=None):
         def step(i):
             at = pl.ds(first + i * 8, 8)
             frm = pl.ds(i * 8, 8)
             n = ORDER[dst]
-            parts[n, at] = (parts[n, at].astype(F32) + src[frm].astype(F32)).astype(BF16)
+            if other is None:
+                parts[n, at] = parts[n, at] + src[frm]
+            else:
+                total = parts[n, at].astype(F32) + src[frm].astype(F32) + other[frm].astype(F32)
+                parts[n, at] = total.astype(BF16)
 
         loop(step, 0, count // 8)
 
     oz_cross = (
-        rcopy(part(1, 3), zq1.at[whole], zm),
-        rcopy(part(2, 3), zq2.at[whole], zp),
+        rcopy(part(1, 3, hi), zq1.at[lo], zm),
+        rcopy(part(2, 3, lo), zq2.at[lo], zp),
     )
     oy_half = {
         j: (
@@ -306,13 +315,36 @@
         )
         for n, j in enumerate((0, 3))
     }
+    oy_side = (
+        rcopy(part(1, 3, lo), ya.at[2], ym),
+        rcopy(part(2, 3, hi), yb.at[2], yp),
+    )
     oy_full = {
         j: (
             rcopy(part(j, 1), yf1.at[j], ym),
             rcopy(part(j, 2), yf2.at[j], yp),
         )
-        for j in range(4)
+        for j in (0,)
     }
+    oy_far = tuple(
+        (
+            rcopy(part(3, 1, blocks), yf1.at[3, blocks], ym),
+            rcopy(part(3, 2, blocks), yf2.at[3, blocks], yp),
+        )
+        for blocks in (lo, hi)
+    )
+    oy_early = (
+        rcopy(part(2, 1), yf1.at[2], ym),
+        rcopy(part(1, 2), yf2.at[1], yp),
+    )
+    oy_next = (
+        rcopy(part(1, 1, hi), yf1.at[1, hi], ym),
+        rcopy(part(2, 2, lo), yf2.at[2, lo], yp),
+    )
+    oy_last = (
+        rcopy(part(1, 1, lo), yf1.at[1, lo], ym),
+        rcopy(part(2, 2, hi), yf2.at[2, hi], yp),
+    )
     oz_half = (
         rcopy(part(3, 0, lo), za.at[lo], zm),
         rcopy(part(3, 0, hi), zb.at[lo], zp),
@@ -322,34 +354,22 @@
         rcopy(part(2, 0), zf2.at[whole], zp),
     )
 
-    def y_mid(j):
-        n = (0, 3).index(j)
-        oy_half[j][0].wait_recv()
-        add_blocks((j, 1), ya.at[n], 0, HALF)
-        oy_full[j][0].start()
-        oy_half[j][1].wait_recv()
-        add_blocks((j, 2), yb.at[n], HALF, HALF)
-        oy_full[j][1].start()
-
-    def y_end(j):
-        arrived(oy_full[j])
-        add_blocks((j, 0), yf1.at[j], 0, DB)
-        add_blocks((j, 0), yf2.at[j], 0, DB)
-
-    y_far[0][0].wait_recv()
-    y_relay_far[0].start()
-    y_far[1][1].wait_recv()
-    y_relay_far[1].start()
-    start(oy_full[1])
-    start(oy_full[2])
+    def y_end(j, first=0, count=DB):
+        at = pl.ds(first, count)
+        add_blocks((j, 0), yf1.at[j, at], first, count, yf2.at[j, at])
+
+    start(oy_early)
+    arrived(z_cross)
     y_far[0][1].wait_recv()
     y_far[1][0].wait_recv()
-    arrived(z_cross)
     arrived(y_relay_far)
     forward(2)
-    spread(10, 6)
-    start(oz_cross)
-    start(oy_half[3])
+    spread(10, 6, 0, DB // 4)
+    oy_half[3][0].start()
+    oz_cross[1].start()
+    spread(10, 6, DB // 4, DB // 2)
+    oy_half[3][1].start()
+    oz_cross[0].start()
 
     steps = (0, 3, 1, 2)
     base = len(copies)
@@ -376,13 +396,13 @@
     def add_core(c):
         core_copy(c).wait_recv()
         for i in (6, 7, 2, 3, 4, 5, 0, 1):
-            wg[0, c, i] = (wg[0, c, i].astype(F32) + core_in[c, i].astype(F32)).astype(BF16)
+            wg[0, c, i] = wg[0, c, i] + core_in[c, i]
         start(x_half(c))
 
     def add_x_half(c):
         arrived(x_half(c))
-        wg[0, c, 2] = (wg[0, c, 2].astype(F32) + xa[c].astype(F32)).astype(BF16)
-        wg[0, c, 5] = (wg[0, c, 5].astype(F32) + xb[c].astype(F32)).astype(BF16)
+        wg[0, c, 2] = wg[0, c, 2] + xa[c]
+        wg[0, c, 5] = wg[0, c, 5] + xb[c]
         start(x_full(c))
 
     def add_x_full(c):
@@ -431,36 +451,70 @@
         def _():
             add_core(c - 1)
 
+        @pl.when(c == 3)
+        def _():
+            oy_half[3][0].wait_recv()
+            add_blocks((3, 1), ya.at[1], 0, HALF)
+            oy_half[3][1].wait_recv()
+            add_blocks((3, 2), yb.at[1], HALF, HALF)
+            start(oy_far[0])
+
         @pl.when(c >= 4)
         def _():
             add_x_half(c - 4)
 
         @pl.when(c == 5)
         def _():
-            y_mid(3)
+            start(oy_far[1])
+
+        @pl.when(c == 7)
+        def _():
+            arrived(oy_far[0])
+            y_end(3, 0, HALF)
+            oz_half[0].start()
 
     loop(weight_grad, 0, COLS)
     add_core(COLS - 1)
+    start(oy_side)
+    start(oy_next)
+    arrived(oz_cross)
+    add_blocks((0, 3), zq1, HALF, HALF)
+    add_blocks((0, 3), zq2, 0, HALF)
+    arrived(oy_far[1])
+    y_end(3, HALF, HALF)
+    oz_half[1].start()
     loop(add_x_half, 4, COLS)
-    y_end(1)
-    y_end(2)
-    arrived(oz_cross)
-    add_blocks((0, 3), zq1, 0, DB)
-    add_blocks((0, 3), zq2, 0, DB)
+    loop(add_x_full, 0, 2)
+    oy_side[0].wait_recv()
+    add_blocks((1, 1), ya.at[2], 0, HALF)
+    oy_last[0].start()
+    oy_side[1].wait_recv()
+    add_blocks((2, 2), yb.at[2], HALF, HALF)
+    oy_last[1].start()
     start(oy_half[0])
-    y_end(3)
-    start(oz_half)
-    loop(add_x_full, 0, 3)
-    y_mid(0)
     oz_half[0].wait_recv()
     add_blocks((1, 0), za, 0, HALF)
+    loop(add_x_full, 2, 4)
+    arrived(oy_early)
+    arrived(oy_next)
+    arrived(oy_last)
+    y_end(1)
     oz_full[0].start()
+    y_end(2)
     oz_half[1].wait_recv()
     add_blocks((2, 0), zb, HALF, HALF)
     oz_full[1].start()
-    loop(add_x_full, 3, COLS)
+    oy_half[0][0].wait_recv()
+    add_blocks((0, 1), ya.at[0], 0, HALF)
+    oy_full[0][0].start()
+    oy_half[0][1].wait_recv()
+    add_blocks((0, 2), yb.at[0], HALF, HALF)
+    oy_full[0][1].start()
+    loop(add_x_full, 4, COLS)
+    loop(finish, 0, 4)
+    arrived(oy_full[0])
     y_end(0)
-    loop(finish, 0, COLS)
+    loop(finish, 4, COLS)
     arrived(oz_full)
     for b in range(DB):
         total = parts[0, b].astype(F32) + zf1[b].astype(F32) + zf2[b].astype(F32)
@@ -521,13 +575,14 @@
             pltpu.VMEM((COLS, 2, *tile), BF16),
             pltpu.VMEM((COLS, 2, *tile), BF16),
             pltpu.VMEM((COLS, *tile), BF16),
-            pltpu.VMEM((2, *half), BF16),
-            pltpu.VMEM((2, *half), BF16),
+            pltpu.VMEM((3, *half), BF16),
+            pltpu.VMEM((3, *half), BF16),
             pltpu.VMEM((4, *full), BF16),
             pltpu.VMEM((4, *full), BF16),
             pltpu.VMEM(half, BF16),
             pltpu.VMEM(half, BF16),
-            *[pltpu.VMEM(full, BF16) for _ in range(4)],
+            *[pltpu.VMEM(full, BF16) for _ in range(2)],
+            *[pltpu.VMEM(half, BF16) for _ in range(2)],
             pltpu.SMEM((COLS, DB), jnp.int32),
             pltpu.SemaphoreType.DMA((2 * SLOTS,)),
             pltpu.SemaphoreType.DMA((COPIES,)),

time: 148 us -> 130 us (0.88)
  Pallas kernels: 145 us -> 127 us
    pallas_call x1, Pallas kernels: 143 us -> 125 us  [body(): pl.pallas_call(functools.partial(kernel, grad_scale), out_shape=shapes, i...]
where the time goes in v3:
time: 130 us; the launch traced here: 128 us
  Pallas kernels  127 us (98%)
    pallas_call x1, Pallas kernels, body(): pl.pallas_call(functools.partial(kernel, grad_scale), out_shape=shapes, i...  125 us

profile of v3, /device:TPU:4, one launch (start us, length us, event | category | flops | bytes accessed | tf_op | source)
XLA Modules:
  0.0 127.9 jit_solution(16903713338943173399)
XLA Ops:
  0.6 124.7 %shard_map.93 = (bf16[24,4096]{1,0:T(8,128)(2,1)}, bf16[24,4096]{1,0:T(8,128)(2,1)}, f32[1,8,128,128]{3,2,1,0:T(8,128)}, f32[1,8,128,128]{3,2,1,0:T(8,128)}) custom-call(s32[8,16]{1,0:T(8,128)} %bitcast.1, s32[8]{0:T(128)} %count_ref.1, bf16[24,4096]{1,0:T(8,128)(2,1)} %tok_ref.1, bf16[24,4096]{1,0:T(8,128)(2,1)} %cot_ref.1, ...), custom_call_target="tpu_custom_call" | custom-call | flops 9663676416 | bytes 12582912 | tf_op jit(solution)/shard_map/pallas_call | solution.py:557
  125.4 2.5 %shard_map.94 = (bf16[24,4096]{1,0:T(8,128)(2,1)}, bf16[24,4096]{1,0:T(8,128)(2,1)}, f32[1,8,128,128]{3,2,1,0:T(8,128)}, f32[1,8,128,128]{3,2,1,0:T(8,128)}) custom-call(bf16[24,4096]{1,0:T(8,128)(2,1)} %get-tuple-element.8.refs_0_, bf16[24,4096]{1,0:T(8,128)(2,1)} %get-tuple-element.9.refs_1_, f32[1,8,128,128]{3,2,1,0:T(8,128)} %get-tuple-element.10.refs_2_, ...), custom_call_target="tpu_custom_call" | custom-call | tf_op jit(solution)/shard_map/pallas_call | solution.py:598

commit v4 on v3

--- a/solution.py
+++ b/solution.py
@@ -349,9 +349,13 @@
         rcopy(part(3, 0, lo), za.at[lo], zm),
         rcopy(part(3, 0, hi), zb.at[lo], zp),
     )
-    oz_full = (
-        rcopy(part(1, 0), zf1.at[whole], zm),
-        rcopy(part(2, 0), zf2.at[whole], zp),
+    oz_first = (
+        rcopy(part(1, 0, hi), zf1.at[hi], zm),
+        rcopy(part(2, 0, lo), zf2.at[lo], zp),
+    )
+    oz_second = (
+        rcopy(part(1, 0, lo), zf1.at[lo], zm),
+        rcopy(part(2, 0, hi), zf2.at[hi], zp),
     )
 
     def y_end(j, first=0, count=DB):
@@ -475,7 +479,6 @@
 
     loop(weight_grad, 0, COLS)
     add_core(COLS - 1)
-    start(oy_side)
     start(oy_next)
     arrived(oz_cross)
     add_blocks((0, 3), zq1, HALF, HALF)
@@ -483,8 +486,16 @@
     arrived(oy_far[1])
     y_end(3, HALF, HALF)
     oz_half[1].start()
-    loop(add_x_half, 4, COLS)
-    loop(add_x_full, 0, 2)
+    start(oy_side)
+    loop(add_x_half, 4, 6)
+    arrived(oy_early)
+    arrived(oy_next)
+    y_end(1, HALF, HALF)
+    oz_first[0].start()
+    y_end(2, 0, HALF)
+    oz_first[1].start()
+    loop(add_x_half, 6, COLS)
+    loop(add_x_full, 0, 1)
     oy_side[0].wait_recv()
     add_blocks((1, 1), ya.at[2], 0, HALF)
     oy_last[0].start()
@@ -494,16 +505,14 @@
     start(oy_half[0])
     oz_half[0].wait_recv()
     add_blocks((1, 0), za, 0, HALF)
-    loop(add_x_full, 2, 4)
-    arrived(oy_early)
-    arrived(oy_next)
-    arrived(oy_last)
-    y_end(1)
-    oz_full[0].start()
-    y_end(2)
     oz_half[1].wait_recv()
     add_blocks((2, 0), zb, HALF, HALF)
-    oz_full[1].start()
+    arrived(oy_last)
+    y_end(1, 0, HALF)
+    oz_second[0].start()
+    y_end(2, HALF, HALF)
+    oz_second[1].start()
+    loop(add_x_full, 1, 4)
     oy_half[0][0].wait_recv()
     add_blocks((0, 1), ya.at[0], 0, HALF)
     oy_full[0][0].start()
@@ -515,7 +524,8 @@
     arrived(oy_full[0])
     y_end(0)
     loop(finish, 4, COLS)
-    arrived(oz_full)
+    arrived(oz_first)
+    arrived(oz_second)
     for b in range(DB):
         total = parts[0, b].astype(F32) + zf1[b].astype(F32) + zf2[b].astype(F32)
         cols = pl.ds(b * BLK, BLK)

time: 130 us -> 127 us (0.977)
  Pallas kernels: 127 us -> 125 us
    pallas_call x1, Pallas kernels: 125 us -> 122 us  [body(): pl.pallas_call(functools.partial(kernel, grad_scale), out_shape=shapes, i...]
where the time goes in v4:
time: 127 us; the launch traced here: 125 us
  Pallas kernels  125 us (98%)
    pallas_call x1, Pallas kernels, body(): pl.pallas_call(functools.partial(kernel, grad_scale), out_shape=shapes, i...  122 us

profile of v4, /device:TPU:4, one launch (start us, length us, event | category | flops | bytes accessed | tf_op | source)
XLA Modules:
  0.0 125.4 jit_solution(8095213445599528815)
XLA Ops:
  0.6 122.2 %shard_map.93 = (bf16[24,4096]{1,0:T(8,128)(2,1)}, bf16[24,4096]{1,0:T(8,128)(2,1)}, f32[1,8,128,128]{3,2,1,0:T(8,128)}, f32[1,8,128,128]{3,2,1,0:T(8,128)}) custom-call(s32[8,16]{1,0:T(8,128)} %bitcast.1, s32[8]{0:T(128)} %count_ref.1, bf16[24,4096]{1,0:T(8,128)(2,1)} %tok_ref.1, bf16[24,4096]{1,0:T(8,128)(2,1)} %cot_ref.1, ...), custom_call_target="tpu_custom_call" | custom-call | flops 9663676416 | bytes 12582912 | tf_op jit(solution)/shard_map/pallas_call | solution.py:567
  122.9 2.5 %shard_map.94 = (bf16[24,4096]{1,0:T(8,128)(2,1)}, bf16[24,4096]{1,0:T(8,128)(2,1)}, f32[1,8,128,128]{3,2,1,0:T(8,128)}, f32[1,8,128,128]{3,2,1,0:T(8,128)}) custom-call(bf16[24,4096]{1,0:T(8,128)(2,1)} %get-tuple-element.8.refs_0_, bf16[24,4096]{1,0:T(8,128)(2,1)} %get-tuple-element.9.refs_1_, f32[1,8,128,128]{3,2,1,0:T(8,128)} %get-tuple-element.10.refs_2_, ...), custom_call_target="tpu_custom_call" | custom-call | tf_op jit(solution)/shard_map/pallas_call | solution.py:608

commit v5 on v4

--- a/solution.py
+++ b/solution.py
@@ -463,10 +463,6 @@
             add_blocks((3, 2), yb.at[1], HALF, HALF)
             start(oy_far[0])
 
-        @pl.when(c >= 4)
-        def _():
-            add_x_half(c - 4)
-
         @pl.when(c == 5)
         def _():
             start(oy_far[1])
@@ -487,7 +483,7 @@
     y_end(3, HALF, HALF)
     oz_half[1].start()
     start(oy_side)
-    loop(add_x_half, 4, 6)
+    loop(add_x_half, 0, 6)
     arrived(oy_early)
     arrived(oy_next)
     y_end(1, HALF, HALF)

time: 127 us -> 126 us (level)
  Pallas kernels: 125 us -> 123 us
where the time goes in v5:
time: 126 us; the launch traced here: 124 us
  Pallas kernels  123 us (98%)
    pallas_call x1, Pallas kernels, body(): pl.pallas_call(functools.partial(kernel, grad_scale), out_shape=shapes, i...  121 us

profile of v5, /device:TPU:4, one launch (start us, length us, event | category | flops | bytes accessed | tf_op | source)
XLA Modules:
  0.0 124.1 jit_solution(8608113977336638758)
XLA Ops:
  0.6 121.0 %shard_map.93 = (bf16[24,4096]{1,0:T(8,128)(2,1)}, bf16[24,4096]{1,0:T(8,128)(2,1)}, f32[1,8,128,128]{3,2,1,0:T(8,128)}, f32[1,8,128,128]{3,2,1,0:T(8,128)}) custom-call(s32[8,16]{1,0:T(8,128)} %bitcast.1, s32[8]{0:T(128)} %count_ref.1, bf16[24,4096]{1,0:T(8,128)(2,1)} %tok_ref.1, bf16[24,4096]{1,0:T(8,128)(2,1)} %cot_ref.1, ...), custom_call_target="tpu_custom_call" | custom-call | flops 9663676416 | bytes 12582912 | tf_op jit(solution)/shard_map/pallas_call | solution.py:563
  121.6 2.5 %shard_map.94 = (bf16[24,4096]{1,0:T(8,128)(2,1)}, bf16[24,4096]{1,0:T(8,128)(2,1)}, f32[1,8,128,128]{3,2,1,0:T(8,128)}, f32[1,8,128,128]{3,2,1,0:T(8,128)}) custom-call(bf16[24,4096]{1,0:T(8,128)(2,1)} %get-tuple-element.8.refs_0_, bf16[24,4096]{1,0:T(8,128)(2,1)} %get-tuple-element.9.refs_1_, f32[1,8,128,128]{3,2,1,0:T(8,128)} %get-tuple-element.10.refs_2_, ...), custom_call_target="tpu_custom_call" | custom-call | tf_op jit(solution)/shard_map/pallas_call | solution.py:604
